TPU v7x, 32 devices: a whole 2x2x4 slice. The times are simulated.
32 devices in a mesh: ty: 8 (over z, y), tx: 4 (over x, core).
Axes of the slice: x: 2, y: 2, z: 4, core: 2. Of those that a mesh axis runs over, the one named last changes fastest.
Arguments:
- object_tiles: float32 [2, 2, 2048, 1024], P(None, None, 'ty', 'tx'), may hold values from -5 to 5
- probe_field: float32 [2, 256, 256], replicated, may hold values from -6 to 6
- prop_angle: float32 [256, 256], replicated, may hold values from -3.140625 to 3.140625
- scan_offsets: int32 [2, 8, 4, 2, 2], P(None, 'ty', 'tx'), may hold values from 0 to 255, as said below
- probe_counts: int32 [2, 8, 4], P(None, 'ty', 'tx'), may hold values from 0 to 2, as said below
- amplitudes: float32 [2, 8, 4, 2, 256, 256], P(None, 'ty', 'tx'), may hold values from 0 to 2.5
Outputs:
- object_out: float32 [2, 2, 2048, 1024], P(None, None, 'ty', 'tx')
Inputs may be any that keep to these rules, and one draw needn't show every extreme that they name: `probe_counts`: every tile has at most 2 live slots in an iteration, and some tile has exactly 2 in every iteration; slots at or past a tile's count are not used. `scan_offsets`: on tiles of the last tile row the row offset is at most 0, and on tiles of the last tile column the column offset is at most 0, so every window lies inside the object.
All inputs are finite; a program needn't handle non-finite values.
Results may differ from a plain program's by a relative error of at most 0.0003.
Values sent between devices are 32-bit elements; how exact they have to be, the bound alone decides.
A program may use at most 128 MiB of HBM per device.

v0:
```python
from functools import partial
import math

import jax
import jax.numpy as jnp
from jax import lax
from jax.sharding import PartitionSpec as P

ITERS = 2


soft_floor = 0.01
step_size = 0.25


def shifted(value, axis, steps):
    count = lax.axis_size(axis)
    first, last = (max(0, -steps), min(count, count - steps))
    return lax.ppermute(value, axis, [(source, source + steps) for source in range(first, last)])


def dft_tables(length):
    index_row = lax.iota(jnp.int32, length)
    phase_index = index_row[:, None] * index_row[None, :] % length
    angles = phase_index.astype(jnp.float32) * (2.0 * math.pi / length)
    norm_factor = 1.0 / math.sqrt(length)
    return (jnp.cos(angles) * norm_factor, -jnp.sin(angles) * norm_factor)


def matmul_high(left_side, right_side):
    return jnp.dot(
        left_side, right_side, precision=lax.Precision.HIGHEST, preferred_element_type=jnp.float32
    )


def local_transform(real_part, imag_part, inverse, tables):
    table_re, table_im = tables
    if inverse:
        table_im = -table_im
    left_re = matmul_high(table_re, real_part) - matmul_high(table_im, imag_part)
    left_im = matmul_high(table_re, imag_part) + matmul_high(table_im, real_part)
    result_re = matmul_high(left_re, table_re) - matmul_high(left_im, table_im)
    result_im = matmul_high(left_re, table_im) + matmul_high(left_im, table_re)
    return (result_re, result_im)


def window_gradient(window, probe_field, kernel_re, kernel_im, measured_amp, transform):
    one_re, one_im = (window[0, 0], window[0, 1])
    two_re, two_im = (window[1, 0], window[1, 1])
    probe_re, probe_im = (probe_field[0], probe_field[1])
    first_re = probe_re * one_re - probe_im * one_im
    first_im = probe_re * one_im + probe_im * one_re
    freq_re, freq_im = transform(first_re, first_im, False)
    moved_re = freq_re * kernel_re - freq_im * kernel_im
    moved_im = freq_re * kernel_im + freq_im * kernel_re
    mid_re, mid_im = transform(moved_re, moved_im, True)
    second_re = mid_re * two_re - mid_im * two_im
    second_im = mid_re * two_im + mid_im * two_re
    far_re, far_im = transform(second_re, second_im, False)
    magnitude = jnp.sqrt(far_re * far_re + far_im * far_im + soft_floor)
    factor = 1.0 - measured_amp / magnitude
    back_re, back_im = transform(far_re * factor, far_im * factor, True)
    grad_two_re = mid_re * back_re + mid_im * back_im
    grad_two_im = mid_re * back_im - mid_im * back_re
    carry_re = two_re * back_re + two_im * back_im
    carry_im = two_re * back_im - two_im * back_re
    spec_re, spec_im = transform(carry_re, carry_im, False)
    turned_re = spec_re * kernel_re + spec_im * kernel_im
    turned_im = spec_im * kernel_re - spec_re * kernel_im
    early_re, early_im = transform(turned_re, turned_im, True)
    grad_one_re = probe_re * early_re + probe_im * early_im
    grad_one_im = probe_re * early_im - probe_im * early_re
    return jnp.stack([jnp.stack([grad_one_re, grad_one_im]), jnp.stack([grad_two_re, grad_two_im])])


def extend_tile(current):
    right_cols = shifted(current, "tx", -1)
    wide_block = jnp.concatenate([current, right_cols], axis=3)
    lower_rows = shifted(wide_block, "ty", -1)
    return jnp.concatenate([wide_block, lower_rows], axis=2)


def return_margins(running, tile_side, probe_side):
    from_left = shifted(running[:, :, :, tile_side:], "tx", 1)
    left_part = running[:, :, :, :tile_side].at[:, :, :, :probe_side].add(from_left)
    from_above = shifted(left_part[:, :, tile_side:, :], "ty", 1)
    return left_part[:, :, :tile_side, :].at[:, :, :probe_side, :].add(from_above)


def shards(object_tiles, probe_field, prop_angle, scan_offsets, probe_counts, amplitudes):
    tile_side = object_tiles.shape[2]
    probe_side = probe_field.shape[1]
    transform = partial(local_transform, tables=dft_tables(probe_side))
    kernel_re = jnp.cos(prop_angle)
    kernel_im = jnp.sin(prop_angle)
    zero_index = jnp.zeros((), jnp.int32)
    current = object_tiles
    for iteration in range(ITERS):
        frozen = extend_tile(current)

        def accumulate(slot_index, running, frozen=frozen, iteration=iteration):
            corner_row = scan_offsets[iteration, 0, 0, slot_index, 0]
            corner_col = scan_offsets[iteration, 0, 0, slot_index, 1]
            start_index = (zero_index, zero_index, corner_row, corner_col)
            window = lax.dynamic_slice(frozen, start_index, (2, 2, probe_side, probe_side))
            measured_amp = amplitudes[iteration, 0, 0, slot_index]
            contrib = window_gradient(
                window, probe_field, kernel_re, kernel_im, measured_amp, transform
            )
            placed = (
                lax.dynamic_slice(running, start_index, (2, 2, probe_side, probe_side)) + contrib
            )
            return lax.dynamic_update_slice(running, placed, start_index)

        extent = tile_side + probe_side
        running = lax.fori_loop(
            0,
            probe_counts[iteration, 0, 0],
            accumulate,
            jnp.zeros((2, 2, extent, extent), jnp.float32),
        )
        gradient = return_margins(running, tile_side, probe_side)
        current = current - step_size * gradient
    return current


def solution(mesh):
    in_specs = (
        P(None, None, "ty", "tx"),
        P(),
        P(),
        P(None, "ty", "tx", None, None),
        P(None, "ty", "tx"),
        P(None, "ty", "tx", None, None, None),
    )
    out_specs = P(None, None, "ty", "tx")
    return jax.shard_map(shards, mesh=mesh, in_specs=in_specs, out_specs=out_specs, check_vma=False)
```

profile of v0, /device:TPU:10, one launch (start us, length us, event | category | flops | bytes accessed | tf_op | source)
XLA Modules:
  0.0 611.0 jit_solution(7604438638327155079)
XLA Ops:
  0.0 2.0 collective-permute-start
  2.1 1.4 constant_dynamic-update-slice_fusion.1
  3.4 11.2 %collective-permute-done = f32[2,2,256,256]{3,2,1,0:T(8,128)S(1)} collective-permute-done((f32[2,2,256,256]{3,2,1,0:T(8,128)}, f32[2,2,256,256]{3,2,1,0:T(8,128)S(1)}, u32[]{:S(2)}, u32[]{:S(2)}) %collective-permute-start) | collective-permute-done | bytes 1048608 | tf_op jit(solution)/shard_map/ppermute | solution.py:19
  14.8 3.3 collective-permute-start.1
  18.1 0.6 fusion.601
  18.7 0.9 fusion.600
  19.7 35.1 %collective-permute-done.1 = f32[2,2,256,512]{3,2,1,0:T(8,128)} collective-permute-done((f32[2,2,256,512]{3,2,1,0:T(8,128)S(1)}, f32[2,2,256,512]{3,2,1,0:T(8,128)}, u32[]{:S(2)}, u32[]{:S(2)}) %collective-permute-start.1) | collective-permute-done | bytes 2097184 | tf_op jit(solution)/shard_map/ppermute | solution.py:19
  54.7 4.0 pad_maximum_fusion
  58.7 2.6 broadcast.187.clone
  61.3 3.4 while.34
  64.7 1.9 slice.176
  66.6 182.7 %collective-permute-start.2 = (f32[2,2,512,256]{3,2,1,0:T(8,128)S(1)}, f32[2,2,512,256]{3,2,1,0:T(8,128)S(1)}, u32[]{:S(2)}, u32[]{:S(2)}) collective-permute-start(f32[2,2,512,256]{3,2,1,0:T(8,128)S(1)} %slice.176), channel_id=1, source_target_pairs={{0,1},{1,2},{2,3},{4,5},{5,6},{6,7},{8,9},{9,10},{10,11},{12,13},{... | collective-permute-start | bytes 6291464 | tf_op jit(solution)/shard_map/ppermute | solution.py:19
  249.2 38.1 %collective-permute-done.2 = f32[2,2,512,256]{3,2,1,0:T(8,128)S(1)} collective-permute-done((f32[2,2,512,256]{3,2,1,0:T(8,128)S(1)}, f32[2,2,512,256]{3,2,1,0:T(8,128)S(1)}, u32[]{:S(2)}, u32[]{:S(2)}) %collective-permute-start.2) | collective-permute-done | bytes 2097184 | tf_op jit(solution)/shard_map/ppermute | solution.py:19
  287.3 0.4 slice_add_fusion.1
  287.8 1.9 collective-permute-start.3
  289.8 15.7 %collective-permute-done.3 = f32[2,2,256,256]{3,2,1,0:T(8,128)S(1)} collective-permute-done((f32[2,2,256,256]{3,2,1,0:T(8,128)S(1)}, f32[2,2,256,256]{3,2,1,0:T(8,128)S(1)}, u32[]{:S(2)}, u32[]{:S(2)}) %collective-permute-start.3) | collective-permute-done | bytes 1048608 | tf_op jit(solution)/shard_map/ppermute | solution.py:19
  305.4 0.2 fusion.599
  305.6 1.9 collective-permute-start.4
  307.6 12.3 %collective-permute-done.4 = f32[2,2,256,256]{3,2,1,0:T(8,128)S(1)} collective-permute-done((f32[2,2,256,256]{3,2,1,0:T(8,128)S(1)}, f32[2,2,256,256]{3,2,1,0:T(8,128)S(1)}, u32[]{:S(2)}, u32[]{:S(2)}) %collective-permute-start.4) | collective-permute-done | bytes 1048608 | tf_op jit(solution)/shard_map/ppermute | solution.py:19
  319.9 1.7 pad_maximum_fusion.2
  321.5 2.0 collective-permute-start.5
  323.6 38.1 %collective-permute-done.5 = f32[2,2,256,512]{3,2,1,0:T(8,128)} collective-permute-done((f32[2,2,256,512]{3,2,1,0:T(8,128)}, f32[2,2,256,512]{3,2,1,0:T(8,128)}, u32[]{:S(2)}, u32[]{:S(2)}) %collective-permute-start.5) | collective-permute-done | bytes 2097184 | tf_op jit(solution)/shard_map/ppermute | solution.py:19
  361.7 4.1 pad_maximum_fusion.1
  365.8 2.6 broadcast.187
  368.3 0.7 while.35
  369.1 1.9 slice.181
  371.0 183.7 %collective-permute-start.6 = (f32[2,2,512,256]{3,2,1,0:T(8,128)S(1)}, f32[2,2,512,256]{3,2,1,0:T(8,128)S(1)}, u32[]{:S(2)}, u32[]{:S(2)}) collective-permute-start(f32[2,2,512,256]{3,2,1,0:T(8,128)S(1)} %slice.181), channel_id=1, source_target_pairs={{0,1},{1,2},{2,3},{4,5},{5,6},{6,7},{8,9},{9,10},{10,11},{12,13},{... | collective-permute-start | bytes 6291464 | tf_op jit(solution)/shard_map/ppermute | solution.py:19
  554.7 3.8 collective-permute-done.6
  558.4 0.4 slice_add_fusion
  558.9 38.5 %collective-permute-start.7 = (f32[2,2,256,256]{3,2,1,0:T(8,128)S(1)}, f32[2,2,256,256]{3,2,1,0:T(8,128)S(1)}, u32[]{:S(2)}, u32[]{:S(2)}) collective-permute-start(f32[2,2,256,256]{3,2,1,0:T(8,128)S(1)} %slice.211), channel_id=1, source_target_pairs={{0,4},{4,8},{8,12},{12,16},{16,20},{20,24},{24,28},{1,5},{5,9},{9,... | collective-permute-start | bytes 3145736 | tf_op jit(solution)/shard_map/ppermute | solution.py:19
  597.5 12.3 %collective-permute-done.7 = f32[2,2,256,256]{3,2,1,0:T(8,128)S(1)} collective-permute-done((f32[2,2,256,256]{3,2,1,0:T(8,128)S(1)}, f32[2,2,256,256]{3,2,1,0:T(8,128)S(1)}, u32[]{:S(2)}, u32[]{:S(2)}) %collective-permute-start.7) | collective-permute-done | bytes 1048608 | tf_op jit(solution)/shard_map/ppermute | solution.py:19
  609.8 1.2 fusion.597
  (17 shorter events, 0.3 us)
Async XLA Ops:
  0.0 18.1 %copy-start.6 = (s32[2,1,1]{0,2,1:T(1,128)S(1)}, s32[2,1,1]{0,2,1:T(1,128)}, u32[]{:S(2)}) copy-start(s32[2,1,1]{0,2,1:T(1,128)} %param.30) | copy-start | bytes 28
  0.0 18.7 %copy-start.4 = (f32[256,256]{1,0:T(8,128)S(1)}, f32[256,256]{1,0:T(8,128)}, u32[]{:S(2)}) copy-start(f32[256,256]{1,0:T(8,128)} %param.28) | copy-start | bytes 786436
  0.0 14.7 %collective-permute-start = (f32[2,2,256,256]{3,2,1,0:T(8,128)}, f32[2,2,256,256]{3,2,1,0:T(8,128)S(1)}, u32[]{:S(2)}, u32[]{:S(2)}) collective-permute-start(f32[2,2,256,256]{3,2,1,0:T(8,128)} %param.26), channel_id=1, source_target_pairs={{1,0},{2,1},{3,2},{5,4},{6,5},{7,6},{9,8},{10,9},{11,10},{13,12},{... | collective-permute-start | bytes 3145736 | tf_op jit(solution)/shard_map/ppermute | solution.py:19
  14.8 39.9 %collective-permute-start.1 = (f32[2,2,256,512]{3,2,1,0:T(8,128)S(1)}, f32[2,2,256,512]{3,2,1,0:T(8,128)}, u32[]{:S(2)}, u32[]{:S(2)}) collective-permute-start(f32[2,2,256,512]{3,2,1,0:T(8,128)S(1)} %constant_dynamic-update-slice_fusion), channel_id=1, source_target_pairs={{4,0},{8,4},{12,8},{16,12},{20,16},{24,20},{28,24},{5,1},{9,5},{13... | collective-permute-start | bytes 6291464 | tf_op jit(solution)/shard_map/ppermute | solution.py:19
  58.7 2.6 copy-start
  58.7 2.6 copy-start.5
  64.6 222.7 %copy-start.2 = (f32[2,2,512,512]{3,2,1,0:T(8,128)S(1)}, f32[2,2,512,512]{3,2,1,0:T(8,128)}, u32[]{:S(2)}) copy-start(f32[2,2,512,512]{3,2,1,0:T(8,128)} %get-tuple-element.571) | copy-start | bytes 12582916
  66.5 238.9 %copy-start.3 = (f32[2,2,256,256]{3,2,1,0:T(8,128)S(1)}, f32[2,2,256,256]{3,2,1,0:T(8,128)}, u32[]{:S(2)}) copy-start(f32[2,2,256,256]{3,2,1,0:T(8,128)} %param.26) | copy-start | bytes 3145732
  66.6 220.8 %collective-permute-start.2 = (f32[2,2,512,256]{3,2,1,0:T(8,128)S(1)}, f32[2,2,512,256]{3,2,1,0:T(8,128)S(1)}, u32[]{:S(2)}, u32[]{:S(2)}) collective-permute-start(f32[2,2,512,256]{3,2,1,0:T(8,128)S(1)} %slice.176), channel_id=1, source_target_pairs={{0,1},{1,2},{2,3},{4,5},{5,6},{6,7},{8,9},{9,10},{10,11},{12,13},{... | collective-permute-start | bytes 6291464 | tf_op jit(solution)/shard_map/ppermute | solution.py:19
  287.8 17.6 %collective-permute-start.3 = (f32[2,2,256,256]{3,2,1,0:T(8,128)S(1)}, f32[2,2,256,256]{3,2,1,0:T(8,128)S(1)}, u32[]{:S(2)}, u32[]{:S(2)}) collective-permute-start(f32[2,2,256,256]{3,2,1,0:T(8,128)S(1)} %slice.209), channel_id=1, source_target_pairs={{0,4},{4,8},{8,12},{12,16},{16,20},{20,24},{24,28},{1,5},{5,9},{9,... | collective-permute-start | bytes 3145736 | tf_op jit(solution)/shard_map/ppermute | solution.py:19
  305.6 14.2 %collective-permute-start.4 = (f32[2,2,256,256]{3,2,1,0:T(8,128)S(1)}, f32[2,2,256,256]{3,2,1,0:T(8,128)S(1)}, u32[]{:S(2)}, u32[]{:S(2)}) collective-permute-start(f32[2,2,256,256]{3,2,1,0:T(8,128)S(1)} %fusion.599), channel_id=1, source_target_pairs={{1,0},{2,1},{3,2},{5,4},{6,5},{7,6},{9,8},{10,9},{11,10},{13,12},{... | collective-permute-start | bytes 3145736 | tf_op jit(solution)/shard_map/ppermute | solution.py:19
  321.5 40.2 %collective-permute-start.5 = (f32[2,2,256,512]{3,2,1,0:T(8,128)}, f32[2,2,256,512]{3,2,1,0:T(8,128)}, u32[]{:S(2)}, u32[]{:S(2)}) collective-permute-start(f32[2,2,256,512]{3,2,1,0:T(8,128)} %pad_maximum_fusion.2), channel_id=1, source_target_pairs={{4,0},{8,4},{12,8},{16,12},{20,16},{24,20},{28,24},{5,1},{9,5},{13... | collective-permute-start | bytes 6291464 | tf_op jit(solution)/shard_map/ppermute | solution.py:19
  369.1 189.4 %copy-start.1 = (f32[2,2,512,512]{3,2,1,0:T(8,128)S(1)}, f32[2,2,512,512]{3,2,1,0:T(8,128)}, u32[]{:S(2)}) copy-start(f32[2,2,512,512]{3,2,1,0:T(8,128)} %get-tuple-element.572) | copy-start | bytes 12582916
  371.0 187.5 %collective-permute-start.6 = (f32[2,2,512,256]{3,2,1,0:T(8,128)S(1)}, f32[2,2,512,256]{3,2,1,0:T(8,128)S(1)}, u32[]{:S(2)}, u32[]{:S(2)}) collective-permute-start(f32[2,2,512,256]{3,2,1,0:T(8,128)S(1)} %slice.181), channel_id=1, source_target_pairs={{0,1},{1,2},{2,3},{4,5},{5,6},{6,7},{8,9},{9,10},{10,11},{12,13},{... | collective-permute-start | bytes 6291464 | tf_op jit(solution)/shard_map/ppermute | solution.py:19
  558.9 50.8 %collective-permute-start.7 = (f32[2,2,256,256]{3,2,1,0:T(8,128)S(1)}, f32[2,2,256,256]{3,2,1,0:T(8,128)S(1)}, u32[]{:S(2)}, u32[]{:S(2)}) collective-permute-start(f32[2,2,256,256]{3,2,1,0:T(8,128)S(1)} %slice.211), channel_id=1, source_target_pairs={{0,4},{4,8},{8,12},{12,16},{16,20},{20,24},{24,28},{1,5},{5,9},{9,... | collective-permute-start | bytes 3145736 | tf_op jit(solution)/shard_map/ppermute | solution.py:19
where the time goes:
time: 617 us; the launch traced here: 611 us
  starting transfers between devices  416 us (67%)
  waiting for transfers between devices  167 us (27%)
  local copies, waits for them, and re-layouts  12.1 us (2%)
  other arithmetic  11.9 us (2%)
    ppermute x8, starting transfers between devices, shifted(): lax.ppermute(value, axis, [(source, source + steps) for source in range(f...  416 us
    ppermute x8, waiting for transfers between devices, shifted(): lax.ppermute(value, axis, [(source, source + steps) for source in range(f...  167 us
  transfers between devices with their start and end apart: 8, of which 8 were waited for; matrix products, arithmetic and copies ran while one was open for 0% of the time, Pallas kernels for 0%

commit v1 on v0

v1 whole, which is shorter than its diff:
```python
import functools
import math

import jax
import jax.numpy as jnp
import ml_dtypes
import numpy as np
from jax import lax
from jax.experimental import pallas as pl
from jax.experimental.pallas import tpu as pltpu
from jax.sharding import PartitionSpec as P

MESH = pl.DeviceIdType.MESH
SOFT_FLOOR = 0.01
STEP_SIZE = 0.25
ROWS = 32
OWN, RIGHT, BELOW, DIAG = range(4)
UP, LEFT, FWD, GOWN, GBELOW, GDOWN = range(6)


def dft_tables(n):
    index = np.arange(n)
    angles = (index[:, None] * index[None, :] % n) * (2.0 * math.pi / n)
    re, im = np.cos(angles) / math.sqrt(n), -np.sin(angles) / math.sqrt(n)

    def terms(table):
        hi = table.astype(np.float32).astype(ml_dtypes.bfloat16)
        return hi, (table - hi.astype(np.float64)).astype(np.float32).astype(ml_dtypes.bfloat16)

    left_hi, left_lo = terms(np.block([[re, -im], [im, re]]))
    right_hi, right_lo = terms(np.block([[re, im], [-im, re]]))
    return (
        np.concatenate([left_hi, left_hi, left_lo], axis=1),
        np.concatenate([right_hi, right_hi, right_lo], axis=0),
    )


def roll_kernel(offsets, probe, rolled):
    iters, slots = rolled.shape[:2]
    for it in range(iters):
        for s in range(slots):
            for part in range(2):
                value = pltpu.roll(probe[part], offsets[it, 0, 0, s, 0], 0)
                rolled[it, s, part] = pltpu.roll(value, offsets[it, 0, 0, s, 1], 1)


def kernel(
    ny, nx, offsets, counts, obj, rolled, prop, amps, left_table, right_table, out,
    cur, halo, grads, got, a_buf, z_buf, b_buf, y_buf, mid_buf, win_buf, send_sem, recv_sem,
):
    n = obj.shape[2]
    iters, slots = rolled.shape[:2]
    ty, tx = lax.axis_index("ty"), lax.axis_index("tx")
    up, down = (lax.rem(ty + ny - 1, ny), tx), (lax.rem(ty + 1, ny), tx)
    left, right = (ty, lax.rem(tx + nx - 1, nx)), (ty, lax.rem(tx + 1, nx))

    barrier = pltpu.get_barrier_semaphore()
    for neighbour in (up, down, left, right):
        pl.semaphore_signal(barrier, inc=1, device_id=neighbour, device_id_type=MESH)
    pl.semaphore_wait(barrier, 4)

    def tile(it, k):
        return obj.at[k // 2, k % 2] if it == 0 else cur.at[k // 2, k % 2]

    def copy(it, kind, k):
        src, dst, target = {
            UP: lambda: (tile(it, k), halo.at[it, BELOW, k], up),
            LEFT: lambda: (tile(it, k), halo.at[it, RIGHT, k], left),
            FWD: lambda: (halo.at[it, BELOW, k], halo.at[it, DIAG, k], left),
            GOWN: lambda: (grads.at[it, RIGHT, k], got.at[it, 0, k], right),
            GBELOW: lambda: (grads.at[it, DIAG, k], got.at[it, 1, k], right),
            GDOWN: lambda: (grads.at[it, BELOW, k], got.at[it, 2, k], down),
        }[kind]()
        return pltpu.make_async_remote_copy(
            src_ref=src, dst_ref=dst, send_sem=send_sem.at[it, kind, k], recv_sem=recv_sem.at[it, kind, k],
            device_id=target, device_id_type=MESH,
        )

    def by_rows(body):
        def step(i, carry):
            body(pl.multiple_of(i * ROWS, ROWS))
            return carry

        lax.fori_loop(0, n // ROWS, step, 0, unroll=2)

    def split(value):
        hi = value.astype(jnp.bfloat16)
        return hi, (value - hi.astype(jnp.float32)).astype(jnp.bfloat16)

    def put(s, row, re, im):
        for part, value in enumerate((re, im)):
            hi, lo = split(value)
            for block, term in ((part, hi), (part + 2, lo), (part + 4, hi)):
                a_buf[pl.ds(block * n + row, ROWS), s * n:(s + 1) * n] = term

    def transform():
        z_buf[...] = jnp.dot(left_table[...], a_buf[...], preferred_element_type=jnp.float32)

        def middle(row):
            for s in range(slots):
                for part in range(2):
                    hi, lo = split(z_buf[pl.ds(part * n + row, ROWS), s * n:(s + 1) * n])
                    for block, term in ((part, hi), (part + 2, lo), (part + 4, hi)):
                        b_buf[pl.ds(s * n + row, ROWS), block * n:(block + 1) * n] = term

        by_rows(middle)
        y_buf[...] = jnp.dot(b_buf[...], right_table[...], preferred_element_type=jnp.float32)

    def result(s, row):
        rows = pl.ds(s * n + row, ROWS)
        return y_buf[rows, :n], y_buf[rows, n:]

    def masks(it, s, row):
        shape = (ROWS, n)
        under = lax.broadcasted_iota(jnp.int32, shape, 0) + row < offsets[it, 0, 0, s, 0]
        beside = lax.broadcasted_iota(jnp.int32, shape, 1) < offsets[it, 0, 0, s, 1]
        return under, beside

    def window(it, s, row, k):
        under, beside = masks(it, s, row)
        rows = pl.ds(row, ROWS)
        inner = jnp.where(beside, halo[it, RIGHT, k, rows, :], tile(it, k)[rows, :])
        outer = jnp.where(beside, halo[it, DIAG, k, rows, :], halo[it, BELOW, k, rows, :])
        return jnp.where(under, outer, inner)

    def place(it, row, k, values):
        rows = pl.ds(row, ROWS)
        sums = [0.0] * 4
        for s, value in enumerate(values):
            under, beside = masks(it, s, row)
            value = value * (s < counts[it, 0, 0]).astype(jnp.float32)
            high, low = jnp.where(under, 0.0, value), jnp.where(under, value, 0.0)
            sums[OWN] += jnp.where(beside, 0.0, high)
            sums[RIGHT] += jnp.where(beside, high, 0.0)
            sums[BELOW] += jnp.where(beside, 0.0, low)
            sums[DIAG] += jnp.where(beside, low, 0.0)
        for quarter in range(4):
            grads[it, quarter, k, rows, :] = sums[quarter]

    def give_right(it, layer):
        for kind in (GBELOW, GOWN):
            for k in (2 * layer, 2 * layer + 1):
                copy(it, kind, k).start()

    def give_down(it, layer):
        for k in (2 * layer, 2 * layer + 1):
            copy(it, GBELOW, k).wait_recv()

            def add(row):
                rows = pl.ds(row, ROWS)
                grads[it, BELOW, k, rows, :] += got[it, 1, k, rows, :]

            by_rows(add)
            copy(it, GDOWN, k).start()

    def update(it, layer):
        last = it == iters - 1
        for k in (2 * layer, 2 * layer + 1):
            copy(it, GOWN, k).wait_recv()
            copy(it, GDOWN, k).wait_recv()

            def step(row):
                rows = pl.ds(row, ROWS)
                total = grads[it, OWN, k, rows, :] + got[it, 0, k, rows, :] + got[it, 2, k, rows, :]
                target = out if last else cur
                target[k // 2, k % 2, rows, :] = tile(it, k)[rows, :] - STEP_SIZE * total

            by_rows(step)
            if not last:
                copy(it + 1, UP, k).start()
                copy(it + 1, LEFT, k).start()

    for k in range(4):
        copy(0, UP, k).start()
        copy(0, LEFT, k).start()

    for it in range(iters):
        for k in ((0, 1, 2, 3) if it == 0 else (2, 3, 0, 1)):
            copy(it, UP, k).wait_recv()
            copy(it, FWD, k).start()
        for k in (0, 1):
            copy(it, LEFT, k).wait_recv()
            copy(it, FWD, k).wait_recv()

        def first(row):
            rows = pl.ds(row, ROWS)
            for s in range(slots):
                re, im = window(it, s, row, 0), window(it, s, row, 1)
                p_re, p_im = rolled[it, s, 0, rows, :], rolled[it, s, 1, rows, :]
                put(s, row, p_re * re - p_im * im, p_re * im + p_im * re)

        by_rows(first)
        transform()

        def propagate(row):
            rows = pl.ds(row, ROWS)
            h_re, h_im = prop[0, rows, :], prop[1, rows, :]
            for s in range(slots):
                re, im = result(s, row)
                put(s, row, re * h_im + im * h_re, re * h_re - im * h_im)

        by_rows(propagate)
        transform()
        for k in (2, 3):
            copy(it, LEFT, k).wait_recv()
            copy(it, FWD, k).wait_recv()

        def second(row):
            rows = pl.ds(row, ROWS)
            for s in range(slots):
                m_im, m_re = result(s, row)
                re, im = window(it, s, row, 2), window(it, s, row, 3)
                mid_buf[s, 0, rows, :], mid_buf[s, 1, rows, :] = m_re, m_im
                win_buf[s, 0, rows, :], win_buf[s, 1, rows, :] = re, im
                put(s, row, m_re * re - m_im * im, m_re * im + m_im * re)

        by_rows(second)
        transform()

        def compare(row):
            rows = pl.ds(row, ROWS)
            for s in range(slots):
                re, im = result(s, row)
                factor = 1.0 - amps[it, 0, 0, s, rows, :] * lax.rsqrt(re * re + im * im + SOFT_FLOOR)
                put(s, row, im * factor, re * factor)

        by_rows(compare)
        transform()

        def back(row):
            rows = pl.ds(row, ROWS)
            found = [[], []]
            for s in range(slots):
                im, re = result(s, row)
                m_re, m_im = mid_buf[s, 0, rows, :], mid_buf[s, 1, rows, :]
                w_re, w_im = win_buf[s, 0, rows, :], win_buf[s, 1, rows, :]
                found[0].append(m_re * re + m_im * im)
                found[1].append(m_re * im - m_im * re)
                put(s, row, w_re * re + w_im * im, w_re * im - w_im * re)
            place(it, row, 2, found[0])
            place(it, row, 3, found[1])

        by_rows(back)
        give_right(it, 1)
        transform()

        def turn(row):
            rows = pl.ds(row, ROWS)
            h_re, h_im = prop[0, rows, :], prop[1, rows, :]
            for s in range(slots):
                re, im = result(s, row)
                put(s, row, im * h_re - re * h_im, re * h_re + im * h_im)

        by_rows(turn)
        transform()

        def early(row):
            rows = pl.ds(row, ROWS)
            found = [[], []]
            for s in range(slots):
                im, re = result(s, row)
                p_re, p_im = rolled[it, s, 0, rows, :], rolled[it, s, 1, rows, :]
                found[0].append(p_re * re + p_im * im)
                found[1].append(p_re * im - p_im * re)
            place(it, row, 0, found[0])
            place(it, row, 1, found[1])

        by_rows(early)
        give_right(it, 0)
        give_down(it, 1)
        give_down(it, 0)
        update(it, 1)
        update(it, 0)

    for it in range(iters):
        for kind in range(6):
            for k in range(4):
                copy(it, kind, k).wait_send()


def shards(ny, nx, object_tiles, probe_field, prop_angle, scan_offsets, probe_counts, amplitudes):
    n = object_tiles.shape[2]
    iters, slots = scan_offsets.shape[0], scan_offsets.shape[3]
    left_table, right_table = dft_tables(n)
    vmem, smem = pl.BlockSpec(memory_space=pltpu.VMEM), pl.BlockSpec(memory_space=pltpu.SMEM)
    rolled = pl.pallas_call(
        roll_kernel,
        out_shape=jax.ShapeDtypeStruct((iters, slots, 2, n, n), jnp.float32),
        in_specs=[smem, vmem],
        out_specs=vmem,
        compiler_params=pltpu.CompilerParams(vmem_limit_bytes=32 * 2**20),
    )(scan_offsets, probe_field)
    prop = jnp.stack([jnp.cos(prop_angle), jnp.sin(prop_angle)])
    f32, bf16 = jnp.float32, jnp.bfloat16
    return pl.pallas_call(
        functools.partial(kernel, ny, nx),
        out_shape=jax.ShapeDtypeStruct(object_tiles.shape, f32),
        in_specs=[smem, smem] + [vmem] * 6,
        out_specs=vmem,
        scratch_shapes=[
            pltpu.VMEM(object_tiles.shape, f32),
            pltpu.VMEM((iters, 4, 4, n, n), f32),
            pltpu.VMEM((iters, 4, 4, n, n), f32),
            pltpu.VMEM((iters, 3, 4, n, n), f32),
            pltpu.VMEM((6 * n, slots * n), bf16),
            pltpu.VMEM((2 * n, slots * n), f32),
            pltpu.VMEM((slots * n, 6 * n), bf16),
            pltpu.VMEM((slots * n, 2 * n), f32),
            pltpu.VMEM((slots, 2, n, n), f32),
            pltpu.VMEM((slots, 2, n, n), f32),
            pltpu.SemaphoreType.DMA((iters, 6, 4)),
            pltpu.SemaphoreType.DMA((iters, 6, 4)),
        ],
        compiler_params=pltpu.CompilerParams(
            collective_id=0, has_side_effects=True, vmem_limit_bytes=56 * 2**20
        ),
    )(scan_offsets, probe_counts, object_tiles, rolled, prop, amplitudes,
      jnp.asarray(left_table), jnp.asarray(right_table))


def solution(mesh):
    in_specs = (
        P(None, None, "ty", "tx"),
        P(),
        P(),
        P(None, "ty", "tx", None, None),
        P(None, "ty", "tx"),
        P(None, "ty", "tx", None, None, None),
    )
    return jax.shard_map(
        functools.partial(shards, mesh.shape["ty"], mesh.shape["tx"]),
        mesh=mesh, in_specs=in_specs, out_specs=P(None, None, "ty", "tx"), check_vma=False,
    )
```

time: 617 us -> 166 us (0.27)
  the two profiles are of different devices: /device:TPU:10 before, /device:TPU:0 now
where the time goes in v1:
time: 166 us
  Pallas kernels  158 us (95%)
  local copies, waits for them, and re-layouts  6.86 us (4%)
    pallas_call x1, Pallas kernels, shards(): pl.pallas_call(functools.partial(kernel, ny, nx), out_shape=jax.ShapeDtyp...  157 us
    unnamed x8, local copies, waits for them, and re-layouts  5 us

profile of v1, /device:TPU:0, one launch (start us, length us, event | category | flops | bytes accessed | tf_op | source)
XLA Modules:
  0.0 165.9 jit_solution(13355466842839879873)
XLA Ops:
  0.0 0.0 copy-start.2
  0.0 0.0 copy-start.1
  0.0 1.4 copy.9.counts
  1.4 1.9 %cosine_bitcast_fusion = (f32[1,256,256]{2,1,0:T(8,128)S(1)}, f32[1,256,256]{2,1,0:T(8,128)S(1)}) fusion(f32[256,256]{1,0:T(8,128)} %param.10), kind=kLoop, calls=%fused_computation.2 | loop fusion | bytes 786432 | tf_op jit(solution)/shard_map/stack | solution.py:293
  3.3 0.8 pad_maximum_fusion.prop
  4.1 0.0 copy-done.2
  4.1 0.0 copy-done.1
  4.1 1.3 shard_map.82.rolled
  5.4 0.0 copy-start
  5.4 1.3 copy-done
  6.8 156.9 %shard_map.83 = f32[2,2,256,256]{3,2,1,0:T(8,128)} custom-call(s32[2,1,1,2,2]{4,3,2,1,0:T(2,128)} %offsets.3, s32[2,1,1]{2,1,0:T(1,128)} %copy.9.counts, f32[2,2,256,256]{3,2,1,0:T(8,128)} %obj.1, f32[2,2,2,256,256]{4,3,2,1,0:T(8,128)} %copy-done, f32[2,256,256]{2,1,0:T(8,128)} %pad_maximum_fusion.prop, f32[2,1,1,2,256,256]{5,4,3,2,1,0:T(8,128)} %amps.1, ...), custom_call_target="tpu_custom_call" | custom-call | tf_op jit(solution)/shard_map/pallas_call | solution.py:295
  163.7 2.3 %copy.11 = f32[2,2,256,256]{3,2,1,0:T(8,128)} copy(f32[2,2,256,256]{3,2,1,0:T(8,128)} %shard_map.83) | data formatting | bytes 2097152
Async XLA Ops:
  0.0 4.1 %copy-start.2 = (s32[2,1,1,2,2]{4,3,2,1,0:T(2,128)S(1)}, s32[2,1,1,2,2]{4,3,2,1,0:T(2,128)}, u32[]{:S(2)}) copy-start(s32[2,1,1,2,2]{4,3,2,1,0:T(2,128)} %offsets.3) | copy-start | bytes 100
  0.0 4.1 %copy-start.1 = (f32[2,256,256]{2,1,0:T(8,128)S(1)}, f32[2,256,256]{2,1,0:T(8,128)}, u32[]{:S(2)}) copy-start(f32[2,256,256]{2,1,0:T(8,128)} %probe.1) | copy-start | bytes 1572868
  5.4 1.3 copy-start

commit v2 on v1

--- a/solution.py
+++ b/solution.py
@@ -35,7 +35,8 @@
     )
 
 
-def roll_kernel(offsets, probe, rolled):
+def prepare_kernel(offsets, probe, angle, rolled, prop):
+    prop[0], prop[1] = jnp.cos(angle[...]), jnp.sin(angle[...])
     iters, slots = rolled.shape[:2]
     for it in range(iters):
         for s in range(slots):
@@ -45,11 +46,20 @@
 
 
 def kernel(
-    ny, nx, offsets, counts, obj, rolled, prop, amps, left_table, right_table, out,
-    cur, halo, grads, got, a_buf, z_buf, b_buf, y_buf, mid_buf, win_buf, send_sem, recv_sem,
+    ny, nx, offsets, counts, obj_hbm, rolled_hbm, prop_hbm, amps_hbm, left_hbm, right_hbm, out,
+    obj, rolled, prop, amps, left_table, right_table, load_sem, cur, halo, grads, got, a_buf, z_buf, b_buf, y_buf, mid_buf, win_buf, send_sem, recv_sem,
 ):
     n = obj.shape[2]
     iters, slots = rolled.shape[:2]
+    loads = [
+        pltpu.make_async_copy(source, target, load_sem.at[i])
+        for i, (source, target) in enumerate((
+            (obj_hbm, obj), (rolled_hbm, rolled), (left_hbm, left_table), (right_hbm, right_table),
+            (prop_hbm, prop), (amps_hbm, amps),
+        ))
+    ]
+    for load in loads:
+        load.start()
     ty, tx = lax.axis_index("ty"), lax.axis_index("tx")
     up, down = (lax.rem(ty + ny - 1, ny), tx), (lax.rem(ty + 1, ny), tx)
     left, right = (ty, lax.rem(tx + nx - 1, nx)), (ty, lax.rem(tx + 1, nx))
@@ -63,9 +73,10 @@
         return obj.at[k // 2, k % 2] if it == 0 else cur.at[k // 2, k % 2]
 
     def copy(it, kind, k):
+        source = obj_hbm.at[k // 2, k % 2] if it == 0 else tile(it, k)
         src, dst, target = {
-            UP: lambda: (tile(it, k), halo.at[it, BELOW, k], up),
-            LEFT: lambda: (tile(it, k), halo.at[it, RIGHT, k], left),
+            UP: lambda: (source, halo.at[it, BELOW, k], up),
+            LEFT: lambda: (source, halo.at[it, RIGHT, k], left),
             FWD: lambda: (halo.at[it, BELOW, k], halo.at[it, DIAG, k], left),
             GOWN: lambda: (grads.at[it, RIGHT, k], got.at[it, 0, k], right),
             GBELOW: lambda: (grads.at[it, DIAG, k], got.at[it, 1, k], right),
@@ -153,34 +164,40 @@
             by_rows(add)
             copy(it, GDOWN, k).start()
 
-    def update(it, layer):
-        last = it == iters - 1
-        for k in (2 * layer, 2 * layer + 1):
-            copy(it, GOWN, k).wait_recv()
-            copy(it, GDOWN, k).wait_recv()
-
-            def step(row):
-                rows = pl.ds(row, ROWS)
-                total = grads[it, OWN, k, rows, :] + got[it, 0, k, rows, :] + got[it, 2, k, rows, :]
-                target = out if last else cur
-                target[k // 2, k % 2, rows, :] = tile(it, k)[rows, :] - STEP_SIZE * total
-
-            by_rows(step)
-            if not last:
-                copy(it + 1, UP, k).start()
-                copy(it + 1, LEFT, k).start()
+    def update(it, k):
+        copy(it, GOWN, k).wait_recv()
+        copy(it, GDOWN, k).wait_recv()
+        target = out if it == iters - 1 else cur
+
+        def step(row):
+            rows = pl.ds(row, ROWS)
+            total = grads[it, OWN, k, rows, :] + got[it, 0, k, rows, :] + got[it, 2, k, rows, :]
+            target[k // 2, k % 2, rows, :] = tile(it, k)[rows, :] - STEP_SIZE * total
+
+        by_rows(step)
+
+    def send(it, k):
+        copy(it, UP, k).start()
+        copy(it, LEFT, k).start()
+
+    def forward(it, k):
+        copy(it, UP, k).wait_recv()
+        copy(it, FWD, k).start()
+
+    def landed(it, k):
+        copy(it, LEFT, k).wait_recv()
+        copy(it, FWD, k).wait_recv()
 
     for k in range(4):
-        copy(0, UP, k).start()
-        copy(0, LEFT, k).start()
+        send(0, k)
+    for load in loads:
+        load.wait()
 
     for it in range(iters):
-        for k in ((0, 1, 2, 3) if it == 0 else (2, 3, 0, 1)):
-            copy(it, UP, k).wait_recv()
-            copy(it, FWD, k).start()
         for k in (0, 1):
-            copy(it, LEFT, k).wait_recv()
-            copy(it, FWD, k).wait_recv()
+            forward(it, k)
+        for k in (0, 1):
+            landed(it, k)
 
         def first(row):
             rows = pl.ds(row, ROWS)
@@ -200,10 +217,11 @@
                 put(s, row, re * h_im + im * h_re, re * h_re - im * h_im)
 
         by_rows(propagate)
-        transform()
+        forward(it, 2)
+        transform()
+        forward(it, 3)
         for k in (2, 3):
-            copy(it, LEFT, k).wait_recv()
-            copy(it, FWD, k).wait_recv()
+            landed(it, k)
 
         def second(row):
             rows = pl.ds(row, ROWS)
@@ -252,6 +270,7 @@
                 put(s, row, im * h_re - re * h_im, re * h_re + im * h_im)
 
         by_rows(turn)
+        give_down(it, 1)
         transform()
 
         def early(row):
@@ -267,10 +286,16 @@
 
         by_rows(early)
         give_right(it, 0)
-        give_down(it, 1)
         give_down(it, 0)
-        update(it, 1)
-        update(it, 0)
+        for k in (2, 3):
+            update(it, k)
+        for k in (0, 1):
+            update(it, k)
+            if it < iters - 1:
+                send(it + 1, k)
+        for k in (2, 3):
+            if it < iters - 1:
+                send(it + 1, k)
 
     for it in range(iters):
         for kind in range(6):
@@ -283,21 +308,30 @@
     iters, slots = scan_offsets.shape[0], scan_offsets.shape[3]
     left_table, right_table = dft_tables(n)
     vmem, smem = pl.BlockSpec(memory_space=pltpu.VMEM), pl.BlockSpec(memory_space=pltpu.SMEM)
-    rolled = pl.pallas_call(
-        roll_kernel,
-        out_shape=jax.ShapeDtypeStruct((iters, slots, 2, n, n), jnp.float32),
-        in_specs=[smem, vmem],
-        out_specs=vmem,
+    rolled, prop = pl.pallas_call(
+        prepare_kernel,
+        out_shape=[
+            jax.ShapeDtypeStruct((iters, slots, 2, n, n), jnp.float32),
+            jax.ShapeDtypeStruct((2, n, n), jnp.float32),
+        ],
+        in_specs=[smem, vmem, vmem],
+        out_specs=[vmem, vmem],
         compiler_params=pltpu.CompilerParams(vmem_limit_bytes=32 * 2**20),
-    )(scan_offsets, probe_field)
-    prop = jnp.stack([jnp.cos(prop_angle), jnp.sin(prop_angle)])
+    )(scan_offsets, probe_field, prop_angle)
     f32, bf16 = jnp.float32, jnp.bfloat16
     return pl.pallas_call(
         functools.partial(kernel, ny, nx),
         out_shape=jax.ShapeDtypeStruct(object_tiles.shape, f32),
-        in_specs=[smem, smem] + [vmem] * 6,
+        in_specs=[smem, smem] + [pl.BlockSpec(memory_space=pltpu.HBM)] * 6,
         out_specs=vmem,
         scratch_shapes=[
+            pltpu.VMEM(object_tiles.shape, f32),
+            pltpu.VMEM(rolled.shape, f32),
+            pltpu.VMEM(prop.shape, f32),
+            pltpu.VMEM(amplitudes.shape, f32),
+            pltpu.VMEM(left_table.shape, bf16),
+            pltpu.VMEM(right_table.shape, bf16),
+            pltpu.SemaphoreType.DMA((6,)),
             pltpu.VMEM(object_tiles.shape, f32),
             pltpu.VMEM((iters, 4, 4, n, n), f32),
             pltpu.VMEM((iters, 4, 4, n, n), f32),

time: 166 us -> 156 us (0.940)
  the two profiles are of different devices: /device:TPU:0 before, /device:TPU:10 now
where the time goes in v2:
time: 156 us; the launch traced here: 155 us
  Pallas kernels  147 us (94%)
  local copies, waits for them, and re-layouts  8.4 us (5%)
    pallas_call x1, Pallas kernels, shards(): pl.pallas_call(functools.partial(kernel, ny, nx), out_shape=jax.ShapeDtyp...  144 us
    unnamed x12, local copies, waits for them, and re-layouts  8.4 us

profile of v2, /device:TPU:10, one launch (start us, length us, event | category | flops | bytes accessed | tf_op | source)
XLA Modules:
  0.0 155.0 jit_solution(11793026191465594462)
XLA Ops:
  0.0 1.3 copy.9.counts
  1.3 0.0 copy-start.1
  1.3 1.0 copy-done.1
  2.4 0.0 copy-start.3
  2.4 0.9 copy-done.3
  3.3 0.0 copy-start.4
  3.3 0.7 copy-done.4
  4.0 2.2 %shard_map.82 = (f32[2,2,2,256,256]{4,3,2,1,0:T(8,128)S(1)}, f32[2,256,256]{2,1,0:T(8,128)S(1)}) custom-call(s32[2,1,1,2,2]{4,3,2,1,0:T(2,128)S(1)} %copy-done.4, f32[2,256,256]{2,1,0:T(8,128)S(1)} %copy-done.1, f32[256,256]{1,0:T(8,128)S(1)} %copy-done.3), custom_call_target="tpu_custom_call" | custom-call | tf_op jit(solution)/shard_map/pallas_call | solution.py:311
  6.2 0.0 copy-start
  6.2 1.3 copy-done
  7.5 0.0 copy-start.2
  7.5 0.8 copy-done.2
  8.3 144.4 %shard_map.83 = f32[2,2,256,256]{3,2,1,0:T(8,128)} custom-call(s32[2,1,1,2,2]{4,3,2,1,0:T(2,128)} %offsets.3, s32[2,1,1]{2,1,0:T(1,128)} %copy.9.counts, f32[2,2,256,256]{3,2,1,0:T(8,128)} %obj_hbm.1, f32[2,2,2,256,256]{4,3,2,1,0:T(8,128)} %copy-done, f32[2,256,256]{2,1,0:T(8,128)} %copy-done.2, f32[2,1,1,2,256,256]{5,4,3,2,1,0:T(8,128)} %amps_hbm.1, ...), custom_call_target="tpu_custom_call" | custom-call | tf_op jit(solution)/shard_map/pallas_call | solution.py:322
  152.8 2.3 %copy.11 = f32[2,2,256,256]{3,2,1,0:T(8,128)} copy(f32[2,2,256,256]{3,2,1,0:T(8,128)} %shard_map.83) | data formatting | bytes 2097152
Async XLA Ops:
  1.3 1.0 copy-start.1
  2.4 0.9 copy-start.3
  3.3 0.7 copy-start.4
  6.2 1.3 copy-start
  7.5 0.8 copy-start.2
